TPU v7x, 32 devices: a whole 2x2x4 slice. The times are simulated.
32 devices in a mesh: pos: 16 (over z, y, x), val: 2 (over core).
Axes of the slice: x: 2, y: 2, z: 4, core: 2. Of those that a mesh axis runs over, the one named last changes fastest.
Arguments:
- send_load: int32 [2, 16], replicated, may hold values from 1 to 16, 64 in all within a row
- tokens: int32 [2, 256, 81], P('val', 'pos'), may hold values from 0 to 63
- owner: int32 [2, 256], P('val', 'pos'), may hold values from 0 to 15
- joint_action: int32 [2, 256, 7], P('val', 'pos'), may hold values from 0 to 31
- board_context: bfloat16 [32, 81, 512], P('pos'), may hold values from -6 to 6
- tok_embed: bfloat16 [64, 512], replicated, may hold values from -6 to 6
- w_qkv: bfloat16 [512, 1536], replicated, may hold values from -0.25 to 0.25
- w_attn_out: bfloat16 [512, 512], replicated, may hold values from -0.25 to 0.25
- w_up: bfloat16 [512, 1024], replicated, may hold values from -0.25 to 0.25
- w_down: bfloat16 [1024, 512], replicated, may hold values from -0.1875 to 0.1875
- w_value: bfloat16 [512, 7], replicated, may hold values from -0.25 to 0.25
Outputs:
- state_values: float32 [2, 256, 7], P('val', 'pos')
- avg_policy: float32 [32, 7, 32], P('pos')
Inputs may be any that keep to these rules, and one draw needn't show every extreme that they name: Each row of send_load sums to 64, and its largest entry is exactly 16.
All inputs are finite; a program needn't handle non-finite values.
Results may differ from a plain program's by a relative error of at most 0.0055.
Values may be sent and summed in bfloat16 or wider, within the bound.
No kernel may reach another device: no remote copies, remote signals or barrier semaphores. Data moves between devices by JAX's collectives and lax.ppermute only.
A program may use at most 64 MiB of HBM per device.

v0:
```python
import functools
import math

import jax
import jax.numpy as jnp
from jax import lax
from jax.experimental import pallas as pl
from jax.experimental.pallas import tpu as pltpu
from jax.sharding import PartitionSpec as P

HEADS = 8
POWERS = 7
ACTIONS = 32
ITERS = 8
SIZES = (5, 6)
LANES = 128
SMOOTHING = 0.01
F32 = jnp.float32
BF16 = jnp.bfloat16


def dot(a, b):
    return jnp.dot(a, b, preferred_element_type=F32)


def dot_nt(a, b):
    return lax.dot_general(a, b, (((1,), (1,)), ((), ())), preferred_element_type=F32)


def dot_tn(a, b):
    return lax.dot_general(a, b, (((0,), (0,)), ((), ())), preferred_element_type=F32)


def norm(u):
    centre = u - jnp.mean(u, axis=-1, keepdims=True)
    spread = jnp.mean(centre * centre, axis=-1, keepdims=True)
    return centre * lax.rsqrt(spread + 1e-05)


def evaluate_kernel(n_rows, n_blocks, locs, *refs):
    load_ref = refs[0]
    owner_refs = refs[1 : 1 + n_blocks]
    token_refs = refs[1 + n_blocks : 1 + 2 * n_blocks]
    (
        board_ref,
        embed_ref,
        value_ref,
        qkv_ref,
        out_ref,
        up_ref,
        down_ref,
    ) = refs[1 + 3 * n_blocks : 8 + 3 * n_blocks]
    result_ref, token_ref, sum_ref = refs[8 + 3 * n_blocks : 11 + 3 * n_blocks]
    scratch = refs[11 + 3 * n_blocks :]
    pos, me = lax.axis_index("pos"), lax.axis_index("val")
    vocab, width = embed_ref.shape
    pitch = -(-locs // 16) * 16
    places = token_ref.shape[0]
    slots = places // n_rows
    starts, total = [], jnp.int32(0)
    for v in range(n_rows):
        starts.append(total)
        total = total + load_ref[v, pos]
    low = lax.div(me * total + (n_rows - 1), jnp.int32(n_rows))
    high = lax.div((me + 1) * total + (n_rows - 1), jnp.int32(n_rows))
    count = high - low

    def block_of(row):
        return lax.rem(row - me + n_rows, n_rows) if n_blocks == 2 else row

    def owner_at(block, slot):
        if n_blocks == 1:
            return owner_refs[0][block, slot]
        return jnp.where(block == 0, owner_refs[0][0, slot], owner_refs[1][0, slot])

    for b in range(n_blocks):
        part = places // n_blocks
        token_ref[b * part : (b + 1) * part, :] = token_refs[b][...]
    sum_ref[...] = jnp.zeros_like(sum_ref)
    for r in (scratch[0], scratch[1], scratch[3]):
        r[...] = jnp.zeros_like(r)
    head = width // HEADS
    pair = 2 * head
    key_gap = jnp.zeros((LANES - pitch, pair), BF16)
    head_gap = jnp.zeros((head, LANES), BF16)
    first_half = lax.broadcasted_iota(jnp.int32, (pitch, pair), 1) < head
    first_scale = jnp.where(first_half, 1.0 / 128.0, 0.0).astype(BF16)
    second_scale = jnp.where(first_half, 0.0, 1.0 / 128.0).astype(BF16)
    row_k = lax.broadcasted_iota(jnp.int32, (2 * LANES, pair), 0)
    lane_k = lax.broadcasted_iota(jnp.int32, (2 * LANES, pair), 1)
    ones_block = jnp.where(
        (lax.rem(row_k, jnp.int32(LANES)) < locs) & ((row_k >= LANES) == (lane_k >= head)), 1.0, 0.0
    ).astype(BF16)
    score_scale = head ** (-0.5) * math.log2(math.e)
    selector_row = lax.broadcasted_iota(jnp.int32, (16, max(SIZES) * pitch), 0)
    selector_lane = lax.broadcasted_iota(jnp.int32, (16, max(SIZES) * pitch), 1)
    vocab_ids = lax.broadcasted_iota(jnp.int32, (vocab, locs), 0)

    def group_step(size, group, carry):
        first = group * size
        state_ref, exact_ref, joined_ref, mixed_ref, normed_ref, hidden_ref = scratch
        rows = slice(0, size * pitch)
        at = []
        selector = jnp.where(
            (lax.div(selector_lane, jnp.int32(pitch)) == selector_row)
            & (lax.rem(selector_lane, jnp.int32(pitch)) < locs),
            1.0,
            0.0,
        ).astype(BF16)[:, rows]

        def embed(g):
            item = low + jnp.minimum(first + g, count - 1)
            row, start = jnp.int32(0), jnp.int32(0)
            for v in range(1, n_rows):
                inside = item >= starts[v]
                row = jnp.where(inside, v, row)
                start = jnp.where(inside, starts[v], start)
            slot = item - start
            block = block_of(row)
            place = block * slots + slot
            at.append(place)
            board = lax.div(owner_at(block, slot), jnp.int32(ITERS))
            ids = token_ref[pl.ds(place, 1), :]
            hot = jnp.where(vocab_ids == ids, 1.0, 0.0).astype(BF16)
            exact = (dot_tn(hot, embed_ref[...]) + board_ref[board]).astype(BF16)
            exact_ref[g * pitch : g * pitch + locs, :] = exact
            state_ref[g * pitch : g * pitch + locs, :] = exact.astype(F32)

        def add_sums(lane, array):
            sums = dot(selector, array)
            for g in range(size):
                sum_ref[pl.ds(at[g], 1), lane : lane + sums.shape[1]] = sums[g : g + 1]

        def norm_state(g):
            here = slice(g * pitch, (g + 1) * pitch)
            normed_ref[here] = norm(state_ref[here]).astype(BF16)

        def join():
            joined_ref[rows] = dot(normed_ref[rows], qkv_ref[...]).astype(BF16)

        def attend(g, p):
            here = slice(g * pitch, (g + 1) * pitch)
            lane = p * pair
            query = joined_ref[here, lane : lane + pair]
            key = joined_ref[here, width + lane : width + lane + pair]
            value = joined_ref[here, 2 * width + lane : 2 * width + lane + pair]
            turned = jnp.concatenate([key, key_gap], axis=0).T
            keys = jnp.concatenate(
                [
                    jnp.concatenate([turned[:head], head_gap], axis=0),
                    jnp.concatenate([head_gap, turned[head:]], axis=0),
                ],
                axis=1,
            )
            values = jnp.concatenate(
                [value * first_scale, key_gap, value * second_scale, key_gap], axis=0
            )
            weights = jnp.exp2(dot(query, keys) * score_scale).astype(BF16)
            both = dot(weights, jnp.concatenate([values, ones_block], axis=1))
            part = (both[:, :pair] / both[:, pair:] * 128.0).astype(BF16)
            mixed_ref[here, lane : lane + pair] = part

        def hide():
            hidden_ref[rows] = state_ref[rows] + dot(mixed_ref[rows], out_ref[...])

        def norm_hidden(g):
            here = slice(g * pitch, (g + 1) * pitch)
            normed_ref[here] = norm(hidden_ref[here]).astype(BF16)

        def feed():
            up = dot(normed_ref[rows], up_ref[...]).astype(BF16)
            inner = up * (
                jnp.asarray(math.sqrt(2.0 / math.pi), BF16)
                + jnp.asarray(math.sqrt(2.0 / math.pi) * 0.044715, BF16) * (up * up)
            )
            half = jnp.asarray(0.5, BF16) * up
            add_sums(2 * width, half + half * jnp.tanh(inner))

        for g in range(size):
            embed(g)
        for g in range(size):
            norm_state(g)
        join()
        for g in range(size):
            for p in range(HEADS // 2):
                attend(g, p)
        hide()
        for g in range(size):
            norm_hidden(g)
        add_sums(0, exact_ref[rows])
        add_sums(width, mixed_ref[rows])
        feed()
        return carry

    small, large = SIZES
    steps = lax.div(count + (large - 1), jnp.int32(large))
    fits = steps * small >= count
    for size, chosen in ((small, fits), (large, jnp.logical_not(fits))):
        lax.fori_loop(0, jnp.where(chosen, steps, 0), functools.partial(group_step, size), 0)
    mixed_active = sum_ref[:, width:]
    upper = mixed_active.astype(BF16)
    halves = jnp.concatenate([upper, (mixed_active - upper.astype(F32)).astype(BF16)], axis=0)
    added = dot(halves[:, :width], out_ref[...]) + dot(halves[:, width:], down_ref[...])
    final = sum_ref[:, :width] + (added[:places] + added[places:])
    pooled = norm(final * (1.0 / locs)).astype(BF16)
    raised = jnp.exp(2.0 * dot_nt(value_ref[...], pooled))
    values = raised / jnp.sum(raised, axis=0, keepdims=True)
    lane = lax.broadcasted_iota(jnp.int32, (POWERS, places), 1)
    mine = lane < 0
    for v in range(n_rows):
        slot = lane - block_of(v) * slots
        item = slot + starts[v]
        mine = mine | (
            (slot >= 0) & (slot < load_ref[v, pos]) & (item >= low) & (item < high)
        )
    result_ref[...] = jnp.where(mine, values, 0.0)


def fetch_kernel(n, *refs):
    sources = refs[:n]
    boards_ref, targets = refs[n], refs[n + 1 : 2 * n]
    board_ref, sem = refs[2 * n :]
    copies = [
        pltpu.make_async_copy(source, target, sem.at[i])
        for i, (source, target) in enumerate(zip(sources, (board_ref,) + targets))
    ]
    for copy in copies:
        copy.start()
    copies[0].wait()
    board = board_ref[...].astype(F32)
    for b in range(boards_ref.shape[0]):
        boards_ref[b] = board[:, b, :]
    for copy in copies[1:]:
        copy.wait()


def finish_kernel(n_rows, n_blocks, *refs):
    load_ref = refs[0]
    owner_refs = refs[1 : 1 + n_blocks]
    action_refs = refs[1 + n_blocks : 1 + 2 * n_blocks]
    value_refs = refs[1 + 2 * n_blocks : 1 + 3 * n_blocks]
    state_values_ref, policy_ref, action_ref, value_ref = refs[1 + 3 * n_blocks :]
    pos, me = lax.axis_index("pos"), lax.axis_index("val")
    slots = state_values_ref.shape[2]
    boards = policy_ref.shape[1]
    places = value_ref.shape[0]
    pad = 8
    lane = lax.broadcasted_iota(jnp.int32, (slots, LANES), 1)
    lane_cell = lax.div(lane, jnp.int32(pad))
    slot_down = lax.broadcasted_iota(jnp.int32, (slots, 1), 0)
    square = lax.broadcasted_iota(jnp.int32, (slots, slots), 0) == lax.broadcasted_iota(
        jnp.int32, (slots, slots), 1
    )
    for v in range(n_rows):
        if n_blocks == 1:
            row = jnp.int32(v)
            owners = owner_refs[0][v : v + 1, :]
            actions = [action_refs[0][i, v : v + 1, :] for i in range(POWERS)]
            values = value_refs[0][:, v * slots : (v + 1) * slots]
        else:
            row = lax.rem(me + v, n_rows)
            owners = owner_refs[v][...]
            actions = [action_refs[v][i] for i in range(POWERS)]
            here, there = v * slots, (1 - v) * slots
            values = (
                value_refs[0][:, here : here + slots] + value_refs[1][:, there : there + slots]
            )

        def store(values=values):
            for i in range(POWERS):
                state_values_ref[i] = values[i : i + 1]

        if n_blocks == 1:
            pl.when(me == v)(store)
        elif v == 0:
            store()
        blank = jnp.zeros((1, slots), F32)
        stacked = jnp.concatenate(
            [values, blank] + [a.astype(F32) for a in actions] + [blank], axis=0
        )
        turned = stacked.T
        cell = jnp.sum(jnp.where(square, owners, 0), axis=1, keepdims=True)
        spread = jnp.concatenate([turned[:, :pad]] * (LANES // pad), axis=1)
        chosen = jnp.concatenate([turned[:, pad:]] * (LANES // pad), axis=1).astype(jnp.int32)
        live = (lane_cell == cell) & (slot_down < load_ref[row, pos])
        action_ref[v * slots : (v + 1) * slots, :] = jnp.where(live, chosen, -1)
        value_ref[v * slots : (v + 1) * slots, :] = spread
    action_ids = lax.broadcasted_iota(jnp.int32, (ACTIONS, LANES), 0)
    unit = 16

    def add_slots(step, sums):
        counts, value_sums = sums
        base = step * unit
        for k in range(unit):
            hit = action_ids == action_ref[pl.ds(base + k, 1), :]
            counts = counts + jnp.where(hit, 1.0, 0.0)
            value_sums = value_sums + jnp.where(hit, value_ref[pl.ds(base + k, 1), :], 0.0)
        return counts, value_sums

    sums = (jnp.zeros((ACTIONS, LANES), F32), jnp.zeros((ACTIONS, LANES), F32))
    if places <= 2 * unit:
        for step in range(places // unit):
            sums = add_slots(step, sums)
    else:
        sums = lax.fori_loop(0, places // unit, add_slots, sums)
    counts, value_sums = sums
    visits = jnp.sum(counts, axis=0, keepdims=True)
    totals = jnp.sum(value_sums, axis=0, keepdims=True)
    baseline = (totals + 1.0 / POWERS) / (visits + 1.0)
    payoff = (value_sums + baseline) / (counts + 1.0)
    regrets = jnp.zeros((ACTIONS, LANES), F32)
    average = jnp.zeros((ACTIONS, LANES), F32)
    for t in range(ITERS):
        positive = jnp.maximum(regrets, 0.0)
        policy = (positive + SMOOTHING) / (
            jnp.sum(positive, axis=0, keepdims=True) + ACTIONS * SMOOTHING
        )
        current = payoff if t == 0 else pltpu.roll(payoff, LANES - t * pad, 1)
        regrets = regrets + current - jnp.sum(policy * current, axis=0, keepdims=True)
        average = average + policy
    turned = (average / ITERS).T
    for b in range(boards):
        first = b * ITERS * pad
        policy_ref[:, b, :] = turned[first : first + POWERS]


def local(
    send_load,
    tokens,
    owner,
    joint_action,
    board_context,
    tok_embed,
    w_qkv,
    w_attn_out,
    w_up,
    w_down,
    w_value,
):
    n_rows = lax.axis_size("val")
    slots, locs = tokens.shape[1:]
    boards = board_context.shape[0]
    width, hidden_units = w_up.shape
    tokens = tokens.reshape(slots, locs)
    actions = jnp.transpose(joint_action, (2, 0, 1))
    if n_rows == 2:

        def rows_of(array, axis):
            return [array, lax.ppermute(array, "val", [(0, 1), (1, 0)])]

    else:

        def rows_of(array, axis):
            return [lax.all_gather(array, "val", axis=axis, tiled=True)]

    token_blocks, owners, actions = rows_of(tokens, 0), rows_of(owner, 0), rows_of(actions, 1)
    n_blocks = len(owners)
    vmem = pl.BlockSpec(memory_space=pltpu.VMEM)
    smem = pl.BlockSpec(memory_space=pltpu.SMEM)
    hbm = pl.BlockSpec(memory_space=pl.ANY)
    rows = max(SIZES) * (-(-locs // 16) * 16)
    places = n_rows * slots
    inputs = (jnp.transpose(board_context, (1, 0, 2)), tok_embed, w_qkv, w_attn_out, w_up, w_down)
    held = pl.pallas_call(
        functools.partial(fetch_kernel, len(inputs)),
        out_shape=[pltpu.VMEM((boards, locs, width), F32)]
        + [pltpu.VMEM(w.shape, BF16) for w in inputs[1:]],
        in_specs=[hbm] * len(inputs),
        out_specs=[vmem] * len(inputs),
        scratch_shapes=[
            pltpu.VMEM(inputs[0].shape, BF16),
            pltpu.SemaphoreType.DMA((len(inputs),)),
        ],
        compiler_params=pltpu.CompilerParams(vmem_limit_bytes=58 * 1024 * 1024),
        cost_estimate=pl.CostEstimate(flops=0, bytes_accessed=9000000, transcendentals=0),
        name="fetch",
    )(*inputs)
    values = pl.pallas_call(
        functools.partial(evaluate_kernel, n_rows, n_blocks, locs),
        out_shape=jax.ShapeDtypeStruct((POWERS, places), F32),
        in_specs=[smem] + [smem] * n_blocks + [vmem] * (2 * n_blocks + 7),
        out_specs=vmem,
        scratch_shapes=[
            pltpu.VMEM((places, locs), jnp.int32),
            pltpu.VMEM((places, 2 * width + hidden_units), F32),
        ]
        + [
            pltpu.VMEM((rows, width), F32),
            pltpu.VMEM((rows, width), BF16),
            pltpu.VMEM((rows, 3 * width), BF16),
            pltpu.VMEM((rows, width), BF16),
            pltpu.VMEM((rows, width), BF16),
            pltpu.VMEM((rows, width), F32),
        ],
        compiler_params=pltpu.CompilerParams(vmem_limit_bytes=28 * 1024 * 1024),
        name="evaluate",
    )(send_load, *owners, *token_blocks, *actions, *held[:2], w_value.T, *held[2:])
    if n_rows == 2:
        shares = [values, lax.ppermute(values, "val", [(0, 1), (1, 0)])]
    else:
        shares = [lax.psum(values, "val")]
    state_values, policy = pl.pallas_call(
        functools.partial(finish_kernel, n_rows, n_blocks),
        out_shape=(
            jax.ShapeDtypeStruct((POWERS, 1, slots), F32),
            jax.ShapeDtypeStruct((POWERS, boards, ACTIONS), F32),
        ),
        in_specs=[smem] + [vmem] * (3 * n_blocks),
        out_specs=(vmem, vmem),
        scratch_shapes=[
            pltpu.VMEM((places, LANES), jnp.int32),
            pltpu.VMEM((places, LANES), F32),
        ],
        compiler_params=pltpu.CompilerParams(vmem_limit_bytes=16 * 1024 * 1024),
        name="finish",
    )(send_load, *owners, *actions, *shares)
    return (jnp.transpose(state_values, (1, 2, 0)), jnp.transpose(policy, (1, 0, 2)))


def solution(mesh):
    in_specs = (
        P(),
        P("val", "pos", None),
        P("val", "pos"),
        P("val", "pos", None),
        P("pos", None, None),
        P(),
        P(),
        P(),
        P(),
        P(),
        P(),
    )
    out_specs = (P("val", "pos", None), P("pos", None, None))
    return jax.shard_map(local, mesh=mesh, in_specs=in_specs, out_specs=out_specs, check_vma=False)
```

profile of v0, /device:TPU:7, one launch (start us, length us, event | category | flops | bytes accessed | tf_op | source)
XLA Modules:
  0.0 17.1 jit_solution(1562564337022702375)
XLA Ops:
  0.6 0.7 %collective-permute-start.2 = (s32[16,81]{1,0:T(8,128)}, s32[16,81]{1,0:T(8,128)S(1)}, u32[]{:S(2)}, u32[]{:S(2)}) collective-permute-start(s32[16,81]{1,0:T(8,128)} %bitcast.9), channel_id=1, source_target_pairs={{0,1},{1,0},{2,3},{3,2},{4,5},{5,4},{6,7},{7,6},{8,9},{9,8},{10,11... | collective-permute-start | bytes 15560 | tf_op jit(solution)/shard_map/ppermute | solution.py:349
  1.4 0.1 collective-permute-start
  1.5 0.4 %collective-permute-start.1 = (s32[7,1,16]{2,1,0:T(1,128)}, s32[7,1,16]{2,1,0:T(1,128)S(1)}, u32[]{:S(2)}, u32[]{:S(2)}) collective-permute-start(s32[7,1,16]{2,1,0:T(1,128)} %bitcast.6), channel_id=1, source_target_pairs={{0,1},{1,0},{2,3},{3,2},{4,5},{5,4},{6,7},{7,6},{8,9},{9,8},{10,11... | collective-permute-start | bytes 1352 | tf_op jit(solution)/shard_map/ppermute | solution.py:349
  1.9 0.0 copy-start
  1.9 0.0 copy-start.1
  1.9 0.0 copy-start.2
  1.9 0.0 copy-start.3
  1.9 0.0 copy-start.4
  1.9 2.4 %fetch.1 = (f32[2,81,512]{2,1,0:T(8,128)S(1)}, bf16[64,512]{1,0:T(8,128)(2,1)S(1)}, bf16[512,1536]{1,0:T(8,128)(2,1)S(1)}, bf16[512,512]{1,0:T(8,128)(2,1)S(1)},...) custom-call(bf16[81,2,512]{2,1,0:T(2,128)(2,1)} %bitcast.12, bf16[64,512]{1,0:T(8,128)(2,1)} %refs_1_.3, ...), custom_call_target="tpu_custom_call" | custom-call | bytes 9000000 | tf_op jit(solution)/shard_map/fetch/pallas_call | solution.py:364
  4.3 0.0 collective-permute-done.refs_2_
  4.3 0.0 collective-permute-done.1.refs_6_.refs_4_
  4.3 0.0 collective-permute-done.2.refs_4_
  4.3 0.0 copy-done
  4.4 0.0 copy-done.1
  4.4 0.0 copy-done.2
  4.4 0.0 copy-done.3
  4.4 0.0 copy-done.4
  4.4 9.6 %evaluate.1.refs_5_ = f32[7,32]{1,0:T(8,128)S(1)} custom-call(s32[2,16]{1,0:T(2,128)S(1)} %copy-done.3, s32[1,16]{1,0:T(1,128)S(1)} %copy-done.4, s32[1,16]{1,0:T(1,128)S(1)} %collective-permute-done.refs_2_, s32[16,81]{1,0:T(8,128)S(1)} %bitcast.10, s32[16,81]{1,0:T(8,128)S(1)} %collective-permute-done.2.refs_4_, s32[7,1,16]{2,1,0:T(1,128)S(1)} %bitcast.7, ...), custom_call_target="tpu_custom_call" | custom-call | tf_op jit(solution)/shard_map/evaluate/pallas_call | solution.py:378
  14.0 0.1 collective-permute-start.3
  14.1 1.1 %collective-permute-done.3.refs_6_ = f32[7,32]{1,0:T(8,128)S(1)} collective-permute-done((f32[7,32]{1,0:T(8,128)S(1)}, f32[7,32]{1,0:T(8,128)S(1)}, u32[]{:S(2)}, u32[]{:S(2)}) %collective-permute-start.3) | collective-permute-done | bytes 928 | tf_op jit(solution)/shard_map/ppermute | solution.py:399
  15.2 1.9 %finish.1 = (f32[7,1,16]{2,1,0:T(1,128)}, f32[7,2,32]{2,1,0:T(2,128)}) custom-call(s32[2,16]{1,0:T(2,128)S(1)} %copy-done.3, s32[1,16]{1,0:T(1,128)S(1)} %copy-done.4, s32[1,16]{1,0:T(1,128)S(1)} %collective-permute-done.refs_2_, s32[7,1,16]{2,1,0:T(1,128)S(1)} %bitcast.8, s32[7,1,16]{2,1,0:T(1,128)S(1)} %collective-permute-done.1.refs_6_.refs_4_, ...), custom_call_target="tpu_custom_call" | custom-call | tf_op jit(solution)/shard_map/finish/pallas_call | solution.py:402
Async XLA Ops:
  0.6 3.7 %collective-permute-start.2 = (s32[16,81]{1,0:T(8,128)}, s32[16,81]{1,0:T(8,128)S(1)}, u32[]{:S(2)}, u32[]{:S(2)}) collective-permute-start(s32[16,81]{1,0:T(8,128)} %bitcast.9), channel_id=1, source_target_pairs={{0,1},{1,0},{2,3},{3,2},{4,5},{5,4},{6,7},{7,6},{8,9},{9,8},{10,11... | collective-permute-start | bytes 15560 | tf_op jit(solution)/shard_map/ppermute | solution.py:349
  1.4 2.9 %collective-permute-start = (s32[1,16]{1,0:T(1,128)}, s32[1,16]{1,0:T(1,128)S(1)}, u32[]{:S(2)}, u32[]{:S(2)}) collective-permute-start(s32[1,16]{1,0:T(1,128)} %refs_1_.5), channel_id=1, source_target_pairs={{0,1},{1,0},{2,3},{3,2},{4,5},{5,4},{6,7},{7,6},{8,9},{9,8},{10,11... | collective-permute-start | bytes 200 | tf_op jit(solution)/shard_map/ppermute | solution.py:349
  1.5 2.9 %collective-permute-start.1 = (s32[7,1,16]{2,1,0:T(1,128)}, s32[7,1,16]{2,1,0:T(1,128)S(1)}, u32[]{:S(2)}, u32[]{:S(2)}) collective-permute-start(s32[7,1,16]{2,1,0:T(1,128)} %bitcast.6), channel_id=1, source_target_pairs={{0,1},{1,0},{2,3},{3,2},{4,5},{5,4},{6,7},{7,6},{8,9},{9,8},{10,11... | collective-permute-start | bytes 1352 | tf_op jit(solution)/shard_map/ppermute | solution.py:349
  1.9 2.5 %copy-start = (s32[1,16,7]{1,0,2:T(1,128)S(1)}, s32[1,16,7]{1,0,2:T(1,128)}, u32[]{:S(2)}) copy-start(s32[1,16,7]{1,0,2:T(1,128)} %param.14) | copy-start | bytes 1348
  1.9 2.5 %copy-start.1 = (s32[1,16,81]{2,1,0:T(8,128)S(1)}, s32[1,16,81]{2,1,0:T(8,128)}, u32[]{:S(2)}) copy-start(s32[1,16,81]{2,1,0:T(8,128)} %param.12) | copy-start | bytes 15556
  1.9 2.5 %copy-start.2 = (bf16[512,7]{0,1:T(8,128)(2,1)S(1)}, bf16[512,7]{0,1:T(8,128)(2,1)}, u32[]{:S(2)}) copy-start(bf16[512,7]{0,1:T(8,128)(2,1)} %param.21) | copy-start | bytes 21508
  1.9 2.5 %copy-start.3 = (s32[2,16]{1,0:T(2,128)S(1)}, s32[2,16]{1,0:T(2,128)}, u32[]{:S(2)}) copy-start(s32[2,16]{1,0:T(2,128)} %refs_0_.3) | copy-start | bytes 388
  1.9 2.5 %copy-start.4 = (s32[1,16]{1,0:T(1,128)S(1)}, s32[1,16]{1,0:T(1,128)}, u32[]{:S(2)}) copy-start(s32[1,16]{1,0:T(1,128)} %refs_1_.5) | copy-start | bytes 196
  14.0 1.2 %collective-permute-start.3 = (f32[7,32]{1,0:T(8,128)S(1)}, f32[7,32]{1,0:T(8,128)S(1)}, u32[]{:S(2)}, u32[]{:S(2)}) collective-permute-start(f32[7,32]{1,0:T(8,128)S(1)} %evaluate.1.refs_5_), channel_id=1, source_target_pairs={{0,1},{1,0},{2,3},{3,2},{4,5},{5,4},{6,7},{7,6},{8,9},{9,8},{10,11... | collective-permute-start | bytes 2696 | tf_op jit(solution)/shard_map/ppermute | solution.py:399
where the time goes:
time: 17.3 us; the launch traced here: 17.1 us
  Pallas kernels  13.9 us (80%)
  starting transfers between devices  1.4 us (8%)
  waiting for transfers between devices  1.09 us (6%)
  between operations  0.72 us (4%)
    pallas_call x1, Pallas kernels, local(): pl.pallas_call(functools.partial(evaluate_kernel, n_rows, n_blocks, locs)...  9.56 us
    pallas_call x1, Pallas kernels, local(): pl.pallas_call(functools.partial(fetch_kernel, len(inputs)), out_shape=[p...  2.4 us
    pallas_call x1, Pallas kernels, local(): pl.pallas_call(functools.partial(finish_kernel, n_rows, n_blocks), out_sh...  1.93 us
    ppermute x3, starting transfers between devices, rows_of(): return [array, lax.ppermute(array, 'val', [(0, 1), (1, 0)])]  1.25 us
    ppermute x1, waiting for transfers between devices, local(): shares = [values, lax.ppermute(values, 'val', [(0, 1), (1, 0)])]  1.08 us
  transfers between devices with their start and end apart: 4, of which 1 were waited for; matrix products, arithmetic and copies ran while one was open for 0% of the time, Pallas kernels for 14%

commit v1 on v0

--- a/solution.py
+++ b/solution.py
@@ -14,6 +14,7 @@
 ITERS = 8
 SIZES = (5, 6)
 LANES = 128
+AHEAD = 8
 SMOOTHING = 0.01
 F32 = jnp.float32
 BF16 = jnp.bfloat16
@@ -77,8 +78,11 @@
         part = places // n_blocks
         token_ref[b * part : (b + 1) * part, :] = token_refs[b][...]
     sum_ref[...] = jnp.zeros_like(sum_ref)
-    for r in (scratch[0], scratch[1], scratch[3]):
-        r[...] = jnp.zeros_like(r)
+    gap = locs // 16 * 16
+    for g in range(max(SIZES)):
+        for r in scratch[:2]:
+            blank = slice(g * pitch + gap, (g + 1) * pitch)
+            r[blank] = jnp.zeros_like(r[blank])
     head = width // HEADS
     pair = 2 * head
     key_gap = jnp.zeros((LANES - pitch, pair), BF16)
@@ -138,12 +142,11 @@
         def join():
             joined_ref[rows] = dot(normed_ref[rows], qkv_ref[...]).astype(BF16)
 
-        def attend(g, p):
+        def score(g, p):
             here = slice(g * pitch, (g + 1) * pitch)
             lane = p * pair
             query = joined_ref[here, lane : lane + pair]
             key = joined_ref[here, width + lane : width + lane + pair]
-            value = joined_ref[here, 2 * width + lane : 2 * width + lane + pair]
             turned = jnp.concatenate([key, key_gap], axis=0).T
             keys = jnp.concatenate(
                 [
@@ -152,10 +155,15 @@
                 ],
                 axis=1,
             )
+            return jnp.exp2(dot(query, keys) * score_scale).astype(BF16)
+
+        def mix(g, p, weights):
+            here = slice(g * pitch, (g + 1) * pitch)
+            lane = p * pair
+            value = joined_ref[here, 2 * width + lane : 2 * width + lane + pair]
             values = jnp.concatenate(
                 [value * first_scale, key_gap, value * second_scale, key_gap], axis=0
             )
-            weights = jnp.exp2(dot(query, keys) * score_scale).astype(BF16)
             both = dot(weights, jnp.concatenate([values, ones_block], axis=1))
             part = (both[:, :pair] / both[:, pair:] * 128.0).astype(BF16)
             mixed_ref[here, lane : lane + pair] = part
@@ -181,9 +189,14 @@
         for g in range(size):
             norm_state(g)
         join()
-        for g in range(size):
-            for p in range(HEADS // 2):
-                attend(g, p)
+        order = [(g, p) for g in range(size) for p in range(HEADS // 2)]
+        waiting = []
+        for here in order + [None] * AHEAD:
+            if here is not None:
+                waiting.append((here, score(*here)))
+            if here is None or len(waiting) > AHEAD:
+                ready, weights = waiting.pop(0)
+                mix(*ready, weights)
         hide()
         for g in range(size):
             norm_hidden(g)
@@ -310,14 +323,15 @@
     payoff = (value_sums + baseline) / (counts + 1.0)
     regrets = jnp.zeros((ACTIONS, LANES), F32)
     average = jnp.zeros((ACTIONS, LANES), F32)
+    payoffs = [payoff] + [pltpu.roll(payoff, LANES - t * pad, 1) for t in range(1, ITERS)]
+    smoothed = [SMOOTHING * jnp.sum(current, axis=0, keepdims=True) for current in payoffs]
     for t in range(ITERS):
+        current = payoffs[t]
         positive = jnp.maximum(regrets, 0.0)
-        policy = (positive + SMOOTHING) / (
-            jnp.sum(positive, axis=0, keepdims=True) + ACTIONS * SMOOTHING
-        )
-        current = payoff if t == 0 else pltpu.roll(payoff, LANES - t * pad, 1)
-        regrets = regrets + current - jnp.sum(policy * current, axis=0, keepdims=True)
-        average = average + policy
+        weight = 1.0 / (jnp.sum(positive, axis=0, keepdims=True) + ACTIONS * SMOOTHING)
+        expected = jnp.sum(positive * current, axis=0, keepdims=True) + smoothed[t]
+        average = average + (positive + SMOOTHING) * weight
+        regrets = regrets + current - expected * weight
     turned = (average / ITERS).T
     for b in range(boards):
         first = b * ITERS * pad
@@ -360,7 +374,7 @@
     hbm = pl.BlockSpec(memory_space=pl.ANY)
     rows = max(SIZES) * (-(-locs // 16) * 16)
     places = n_rows * slots
-    inputs = (jnp.transpose(board_context, (1, 0, 2)), tok_embed, w_qkv, w_attn_out, w_up, w_down)
+    inputs = (jnp.transpose(board_context, (1, 0, 2)), tok_embed, w_qkv, w_attn_out)
     held = pl.pallas_call(
         functools.partial(fetch_kernel, len(inputs)),
         out_shape=[pltpu.VMEM((boards, locs, width), F32)]
@@ -394,7 +408,7 @@
         ],
         compiler_params=pltpu.CompilerParams(vmem_limit_bytes=28 * 1024 * 1024),
         name="evaluate",
-    )(send_load, *owners, *token_blocks, *actions, *held[:2], w_value.T, *held[2:])
+    )(send_load, *owners, *token_blocks, *actions, *held[:2], w_value.T, *held[2:], w_up, w_down)
     if n_rows == 2:
         shares = [values, lax.ppermute(values, "val", [(0, 1), (1, 0)])]
     else:

time: 17.3 us -> 15.3 us (0.88)
  the two profiles are of different devices: /device:TPU:7 before, /device:TPU:23 now
where the time goes in v1:
time: 15.3 us; the launch traced here: 15.6 us
  Pallas kernels  11.4 us (75%)
  starting transfers between devices  2.46 us (16%)
  waiting for transfers between devices  0.83 us (5%)
  between operations  0.78 us (5%)
    pallas_call x1, Pallas kernels, local(): pl.pallas_call(functools.partial(evaluate_kernel, n_rows, n_blocks, locs)...  7.9 us
    pallas_call x1, Pallas kernels, local(): pl.pallas_call(functools.partial(finish_kernel, n_rows, n_blocks), out_sh...  1.88 us
    pallas_call x1, Pallas kernels, local(): pl.pallas_call(functools.partial(fetch_kernel, len(inputs)), out_shape=[p...  1.67 us
    ppermute x3, starting transfers between devices, rows_of(): return [array, lax.ppermute(array, 'val', [(0, 1), (1, 0)])]  1.25 us
    ppermute x1, starting transfers between devices, local(): shares = [values, lax.ppermute(values, 'val', [(0, 1), (1, 0)])]  1.21 us
    ppermute x1, waiting for transfers between devices, local(): shares = [values, lax.ppermute(values, 'val', [(0, 1), (1, 0)])]  0.82 us
  transfers between devices with their start and end apart: 4, of which 1 were waited for; matrix products, arithmetic and copies ran while one was open for 0% of the time, Pallas kernels for 11%

profile of v1, /device:TPU:23, one launch (start us, length us, event | category | flops | bytes accessed | tf_op | source)
XLA Modules:
  0.0 15.6 jit_solution(3595403241507167146)
XLA Ops:
  0.6 0.0 copy-start.3
  0.6 0.0 copy-start.2
  0.7 0.0 copy-start.6
  0.7 0.0 copy-start.5
  0.7 0.0 copy-start.4
  0.7 0.0 copy-start.1
  0.7 0.0 copy-start
  0.7 0.7 %collective-permute-start.2 = (s32[16,81]{1,0:T(8,128)}, s32[16,81]{1,0:T(8,128)S(1)}, u32[]{:S(2)}, u32[]{:S(2)}) collective-permute-start(s32[16,81]{1,0:T(8,128)} %bitcast.9), channel_id=1, source_target_pairs={{0,1},{1,0},{2,3},{3,2},{4,5},{5,4},{6,7},{7,6},{8,9},{9,8},{10,11... | collective-permute-start | bytes 15560 | tf_op jit(solution)/shard_map/ppermute | solution.py:363
  1.4 0.1 collective-permute-start.1
  1.5 0.4 %collective-permute-start = (s32[1,16]{1,0:T(1,128)}, s32[1,16]{1,0:T(1,128)S(1)}, u32[]{:S(2)}, u32[]{:S(2)}) collective-permute-start(s32[1,16]{1,0:T(1,128)} %refs_1_.5), channel_id=1, source_target_pairs={{0,1},{1,0},{2,3},{3,2},{4,5},{5,4},{6,7},{7,6},{8,9},{9,8},{10,11... | collective-permute-start | bytes 200 | tf_op jit(solution)/shard_map/ppermute | solution.py:363
  2.0 1.7 %fetch.1 = (f32[2,81,512]{2,1,0:T(8,128)S(1)}, bf16[64,512]{1,0:T(8,128)(2,1)S(1)}, bf16[512,1536]{1,0:T(8,128)(2,1)S(1)}, bf16[512,512]{1,0:T(8,128)(2,1)S(1)}) custom-call(bf16[81,2,512]{2,1,0:T(2,128)(2,1)} %bitcast.12, bf16[64,512]{1,0:T(8,128)(2,1)} %refs_1_.3, bf16[512,1536]{1,0:T(8,128)(2,1)} %refs_2_.1, bf16[512,512]{1,0:T(8,128)(2,1)} %refs_3_.1), custom_call_target="tpu_custom_call" | custom-call | bytes 9000000 | tf_op jit(solution)/shard_map/fetch/pallas_call | solution.py:378
  3.6 0.0 collective-permute-done.refs_2_
  3.6 0.0 collective-permute-done.1.refs_6_.refs_4_
  3.7 0.0 collective-permute-done.2.refs_4_
  3.7 0.0 copy-done.3
  3.7 0.0 copy-done.2
  3.7 0.0 copy-done.6
  3.7 0.0 copy-done.5
  3.7 0.0 copy-done.4
  3.7 0.0 copy-done.1
  3.7 0.0 copy-done
  3.7 7.9 %evaluate.1.refs_5_ = f32[7,32]{1,0:T(8,128)S(1)} custom-call(s32[2,16]{1,0:T(2,128)S(1)} %copy-done.5, s32[1,16]{1,0:T(1,128)S(1)} %copy-done.6, s32[1,16]{1,0:T(1,128)S(1)} %collective-permute-done.refs_2_, s32[16,81]{1,0:T(8,128)S(1)} %bitcast.10, s32[16,81]{1,0:T(8,128)S(1)} %collective-permute-done.2.refs_4_, s32[7,1,16]{2,1,0:T(1,128)S(1)} %bitcast.7, ...), custom_call_target="tpu_custom_call" | custom-call | tf_op jit(solution)/shard_map/evaluate/pallas_call | solution.py:392
  11.6 1.2 %collective-permute-start.3 = (f32[7,32]{1,0:T(8,128)S(1)}, f32[7,32]{1,0:T(8,128)S(1)}, u32[]{:S(2)}, u32[]{:S(2)}) collective-permute-start(f32[7,32]{1,0:T(8,128)S(1)} %evaluate.1.refs_5_), channel_id=1, source_target_pairs={{0,1},{1,0},{2,3},{3,2},{4,5},{5,4},{6,7},{7,6},{8,9},{9,8},{10,11... | collective-permute-start | bytes 2696 | tf_op jit(solution)/shard_map/ppermute | solution.py:413
  12.8 0.8 %collective-permute-done.3.refs_6_ = f32[7,32]{1,0:T(8,128)S(1)} collective-permute-done((f32[7,32]{1,0:T(8,128)S(1)}, f32[7,32]{1,0:T(8,128)S(1)}, u32[]{:S(2)}, u32[]{:S(2)}) %collective-permute-start.3) | collective-permute-done | bytes 928 | tf_op jit(solution)/shard_map/ppermute | solution.py:413
  13.7 1.9 %finish.1 = (f32[7,1,16]{2,1,0:T(1,128)}, f32[7,2,32]{2,1,0:T(2,128)}) custom-call(s32[2,16]{1,0:T(2,128)S(1)} %copy-done.5, s32[1,16]{1,0:T(1,128)S(1)} %copy-done.6, s32[1,16]{1,0:T(1,128)S(1)} %collective-permute-done.refs_2_, s32[7,1,16]{2,1,0:T(1,128)S(1)} %bitcast.8, s32[7,1,16]{2,1,0:T(1,128)S(1)} %collective-permute-done.1.refs_6_.refs_4_, ...), custom_call_target="tpu_custom_call" | custom-call | tf_op jit(solution)/shard_map/finish/pallas_call | solution.py:416
Async XLA Ops:
  0.6 3.0 %copy-start.3 = (s32[1,16,81]{2,1,0:T(8,128)S(1)}, s32[1,16,81]{2,1,0:T(8,128)}, u32[]{:S(2)}) copy-start(s32[1,16,81]{2,1,0:T(8,128)} %param.12) | copy-start | bytes 15556
  0.6 3.0 %copy-start.2 = (s32[1,16,7]{1,0,2:T(1,128)S(1)}, s32[1,16,7]{1,0,2:T(1,128)}, u32[]{:S(2)}) copy-start(s32[1,16,7]{1,0,2:T(1,128)} %param.14) | copy-start | bytes 1348
  0.7 3.0 %copy-start.6 = (s32[1,16]{1,0:T(1,128)S(1)}, s32[1,16]{1,0:T(1,128)}, u32[]{:S(2)}) copy-start(s32[1,16]{1,0:T(1,128)} %refs_1_.5) | copy-start | bytes 196
  0.7 3.0 %copy-start.5 = (s32[2,16]{1,0:T(2,128)S(1)}, s32[2,16]{1,0:T(2,128)}, u32[]{:S(2)}) copy-start(s32[2,16]{1,0:T(2,128)} %refs_0_.3) | copy-start | bytes 388
  0.7 3.0 %copy-start.4 = (bf16[512,7]{0,1:T(8,128)(2,1)S(1)}, bf16[512,7]{0,1:T(8,128)(2,1)}, u32[]{:S(2)}) copy-start(bf16[512,7]{0,1:T(8,128)(2,1)} %param.21) | copy-start | bytes 21508
  0.7 3.0 %copy-start.1 = (bf16[1024,512]{1,0:T(8,128)(2,1)S(1)}, bf16[1024,512]{1,0:T(8,128)(2,1)}, u32[]{:S(2)}) copy-start(bf16[1024,512]{1,0:T(8,128)(2,1)} %refs_13_.1) | copy-start | bytes 3145732
  0.7 3.0 %copy-start = (bf16[512,1024]{1,0:T(8,128)(2,1)S(1)}, bf16[512,1024]{1,0:T(8,128)(2,1)}, u32[]{:S(2)}) copy-start(bf16[512,1024]{1,0:T(8,128)(2,1)} %refs_12_.1) | copy-start | bytes 3145732
  0.7 3.0 %collective-permute-start.2 = (s32[16,81]{1,0:T(8,128)}, s32[16,81]{1,0:T(8,128)S(1)}, u32[]{:S(2)}, u32[]{:S(2)}) collective-permute-start(s32[16,81]{1,0:T(8,128)} %bitcast.9), channel_id=1, source_target_pairs={{0,1},{1,0},{2,3},{3,2},{4,5},{5,4},{6,7},{7,6},{8,9},{9,8},{10,11... | collective-permute-start | bytes 15560 | tf_op jit(solution)/shard_map/ppermute | solution.py:363
  1.4 2.2 %collective-permute-start.1 = (s32[7,1,16]{2,1,0:T(1,128)}, s32[7,1,16]{2,1,0:T(1,128)S(1)}, u32[]{:S(2)}, u32[]{:S(2)}) collective-permute-start(s32[7,1,16]{2,1,0:T(1,128)} %bitcast.6), channel_id=1, source_target_pairs={{0,1},{1,0},{2,3},{3,2},{4,5},{5,4},{6,7},{7,6},{8,9},{9,8},{10,11... | collective-permute-start | bytes 1352 | tf_op jit(solution)/shard_map/ppermute | solution.py:363
  1.5 2.1 %collective-permute-start = (s32[1,16]{1,0:T(1,128)}, s32[1,16]{1,0:T(1,128)S(1)}, u32[]{:S(2)}, u32[]{:S(2)}) collective-permute-start(s32[1,16]{1,0:T(1,128)} %refs_1_.5), channel_id=1, source_target_pairs={{0,1},{1,0},{2,3},{3,2},{4,5},{5,4},{6,7},{7,6},{8,9},{9,8},{10,11... | collective-permute-start | bytes 200 | tf_op jit(solution)/shard_map/ppermute | solution.py:363
  11.6 2.0 %collective-permute-start.3 = (f32[7,32]{1,0:T(8,128)S(1)}, f32[7,32]{1,0:T(8,128)S(1)}, u32[]{:S(2)}, u32[]{:S(2)}) collective-permute-start(f32[7,32]{1,0:T(8,128)S(1)} %evaluate.1.refs_5_), channel_id=1, source_target_pairs={{0,1},{1,0},{2,3},{3,2},{4,5},{5,4},{6,7},{7,6},{8,9},{9,8},{10,11... | collective-permute-start | bytes 2696 | tf_op jit(solution)/shard_map/ppermute | solution.py:413
